TPU v7x, 32 devices: a whole 2x2x4 slice. The times are simulated.
32 devices in a mesh: groups: 2 (over y), req: 4 (over x, core), tensor: 4 (over z).
Axes of the slice: x: 2, y: 2, z: 4, core: 2. Of those that a mesh axis runs over, the one named last changes fastest.
Arguments:
- hidden: bfloat16 [384, 24576], P(('groups', 'req'), 'tensor'), parts along dimension 0, may hold values from -6 to 6
- join_weight: bfloat16 [24576, 8192], P('tensor', 'req'), may hold values from -0.0390625 to 0.0390625
- norm_gain: bfloat16 [8192], P(('req', 'tensor')), may hold values from 0.099609375 to 1.8984375
- qkv_weight: bfloat16 [8192, 9216], P(('req', 'tensor')), may hold values from -0.0625 to 0.0625
- owner_draft_cache: bfloat16 [48, 512, 2, 512], P(('groups', 'req'), 'tensor'), parts along dimension 0, may hold values from -250 to 250
- node_count: int32 [48], P('groups'), parts along dimension 0, may hold values from 1 to 8, as said below
- owner: int32 [48], P('groups'), parts along dimension 0, may hold values from 0 to 3, as said below
- cache_len: int32 [48], P('groups'), parts along dimension 0, may hold values from 1 to 512, as said below
Outputs:
- draft_attention: bfloat16 [48, 8, 8192], P(('groups', 'req'), None, 'tensor'), parts along dimension 0
There are 2 independent parts, one for each index of `groups`. A program takes and returns all parts, laid end to end along the dimension named above; an argument that names none is the same for every part. Nothing has to cross between parts.
Inputs may be any that keep to these rules, and one draw needn't show every extreme that they name: Every owner holds exactly 6 requests. `node_count`: some request has all 8 nodes live. `cache_len`: some slot uses all 512 positions.
All inputs are finite; a program needn't handle non-finite values.
Results may differ from a plain program's by a relative error of at most 0.01655.
The roundings to bfloat16 on the way count: a program that leaves them out, or rounds other values in their place, can miss the bound.
Values may be sent and summed in bfloat16 or wider, within the bound.
A program may use at most 256 MiB of HBM per device.

v0:
```python
import jax
import jax.numpy as jnp
from jax import lax
from jax.sharding import PartitionSpec as P

DF = 8192
QUERY_HEADS = 64
KEY_VALUE_HEADS = 4
HEAD_SIZE = 128
TREE_SLOTS = 8
CACHE_BLOCK = 128
norm_eps = 1e-05


def slots(owner, request_per_owner):
    count_all = owner.shape[0]
    same_owner = owner[:, None] == owner[None, :]
    earlier = jnp.arange(count_all)[None, :] < jnp.arange(count_all)[:, None]
    ranking = jnp.sum((same_owner & earlier).astype(jnp.int32), axis=1)
    return owner * request_per_owner + ranking


def body(
    hidden, join_weight, norm_gain, qkv_weight, owner_draft_cache, node_count, owner, cache_len
):
    tensor_count = lax.axis_size("tensor")
    req_here = lax.axis_index("req")
    tensor_here = lax.axis_index("tensor")
    request_per_owner = owner_draft_cache.shape[0]
    count_all = owner.shape[0]
    slot_of = slots(owner, request_per_owner)
    slot_table = slot_of[None, :] == jnp.arange(count_all, dtype=jnp.int32)[:, None]
    rows_all = count_all * TREE_SLOTS
    hidden_all = lax.all_gather(hidden, "req", axis=0, tiled=True)
    partial_sum = jnp.dot(hidden_all, join_weight, preferred_element_type=jnp.float32)
    joined = lax.psum_scatter(partial_sum, "tensor", scatter_dimension=1, tiled=True).astype(
        jnp.bfloat16
    )
    features = joined.shape[1]
    joined = jnp.dot(
        slot_table.astype(jnp.bfloat16),
        joined.reshape(count_all, TREE_SLOTS * features),
        preferred_element_type=jnp.float32,
    ).reshape(rows_all, features)
    scaled = (joined * norm_gain.astype(jnp.float32)).astype(jnp.bfloat16)
    partial_qkv = jnp.dot(scaled, qkv_weight, preferred_element_type=jnp.float32)
    row_squares = jnp.sum(joined * joined, axis=1)
    own_qkv = lax.psum_scatter(partial_qkv, "req", scatter_dimension=0, tiled=True)
    total_squares = lax.dynamic_slice_in_dim(
        lax.psum(row_squares, ("req", "tensor")),
        req_here * request_per_owner * TREE_SLOTS,
        request_per_owner * TREE_SLOTS,
    )
    total_qkv = lax.psum(own_qkv, "tensor")
    query_key_value = (total_qkv * lax.rsqrt(total_squares[:, None] / DF + norm_eps)).astype(
        jnp.bfloat16
    )
    query_group_width = QUERY_HEADS // KEY_VALUE_HEADS
    query_rows = query_key_value[:, : QUERY_HEADS * HEAD_SIZE].reshape(
        request_per_owner, TREE_SLOTS, KEY_VALUE_HEADS, query_group_width, HEAD_SIZE
    )
    fresh_key = query_key_value[
        :, QUERY_HEADS * HEAD_SIZE : (QUERY_HEADS + KEY_VALUE_HEADS) * HEAD_SIZE
    ].reshape(request_per_owner, TREE_SLOTS, KEY_VALUE_HEADS, HEAD_SIZE)
    fresh_value = query_key_value[:, (QUERY_HEADS + KEY_VALUE_HEADS) * HEAD_SIZE :].reshape(
        request_per_owner, TREE_SLOTS, KEY_VALUE_HEADS, HEAD_SIZE
    )
    cached_key_rows = owner_draft_cache[:, :, 0].reshape(
        request_per_owner, CACHE_BLOCK, KEY_VALUE_HEADS, HEAD_SIZE
    )
    cached_value_rows = owner_draft_cache[:, :, 1].reshape(
        request_per_owner, CACHE_BLOCK, KEY_VALUE_HEADS, HEAD_SIZE
    )
    lengths = lax.dynamic_slice_in_dim(cache_len, req_here * request_per_owner, request_per_owner)
    live_all = jnp.sum(jnp.where(slot_table, node_count[None, :], 0), axis=1)
    live_slot = lax.dynamic_slice_in_dim(live_all, req_here * request_per_owner, request_per_owner)
    scale_factor = HEAD_SIZE ** (-0.5)
    positions = tensor_here * CACHE_BLOCK + jnp.arange(CACHE_BLOCK)
    cache_mask = (positions[None, :] < lengths[:, None])[:, None, None, None, :]
    score_cache = (
        jnp.einsum(
            "snkgd,spkd->snkgp", query_rows, cached_key_rows, preferred_element_type=jnp.float32
        )
        * scale_factor
    )
    score_cache = jnp.where(cache_mask, score_cache, -1e30)
    first_block = tensor_here == 0
    new_mask = (jnp.arange(TREE_SLOTS)[None, :] <= jnp.arange(TREE_SLOTS)[:, None]) & first_block
    new_mask = new_mask[None, :, None, None, :]
    score_new = (
        jnp.einsum("snkgd,smkd->snkgm", query_rows, fresh_key, preferred_element_type=jnp.float32)
        * scale_factor
    )
    score_new = jnp.where(new_mask, score_new, -1e30)
    local_top = jnp.maximum(jnp.max(score_cache, axis=-1), jnp.max(score_new, axis=-1))
    top_score = lax.pmax(local_top, "tensor")
    weight_cache = jnp.where(cache_mask, jnp.exp(score_cache - top_score[..., None]), 0.0)
    weight_new = jnp.where(new_mask, jnp.exp(score_new - top_score[..., None]), 0.0)
    denominator = jnp.sum(weight_cache, axis=-1) + jnp.sum(weight_new, axis=-1)
    accum = jnp.einsum(
        "snkgp,spkd->snkgd",
        weight_cache.astype(jnp.bfloat16),
        cached_value_rows,
        preferred_element_type=jnp.float32,
    )
    accum = accum + jnp.einsum(
        "snkgm,smkd->snkgd",
        weight_new.astype(jnp.bfloat16),
        fresh_value,
        preferred_element_type=jnp.float32,
    )
    head_cols = QUERY_HEADS * HEAD_SIZE // tensor_count
    accum_all, denom_all = lax.psum((accum, denominator), "tensor")
    result_all = (accum_all / denom_all[..., None]).reshape(
        request_per_owner, TREE_SLOTS, QUERY_HEADS * HEAD_SIZE
    )
    result = lax.dynamic_slice_in_dim(result_all, tensor_here * head_cols, head_cols, 2)
    alive = (jnp.arange(TREE_SLOTS)[None, :] < live_slot[:, None])[:, :, None]
    return jnp.where(alive, result, 0.0).astype(jnp.bfloat16)


def solution(mesh):
    return jax.shard_map(
        body,
        mesh=mesh,
        in_specs=(
            P(("groups", "req"), "tensor"),
            P("tensor", "req"),
            P(("req", "tensor")),
            P(("req", "tensor"), None),
            P(("groups", "req"), "tensor", None, None),
            P("groups"),
            P("groups"),
            P("groups"),
        ),
        out_specs=P(("groups", "req"), None, "tensor"),
        check_vma=False,
    )
```

profile of v0, /device:TPU:0, one launch (start us, length us, event | category | flops | bytes accessed | tf_op | source)
XLA Modules:
  0.0 341.3 jit_solution(7624498871045635591)
XLA Ops:
  6.5 0.7 all-gather.2.cloned.1.call-update
  7.3 28.4 %all-gather.2.cloned.1.call-done = bf16[192,6144]{1,0:T(8,128)(2,1)} async-done(((bf16[48,6144]{1,0:T(8,128)(2,1)}), bf16[192,6144]{1,0:T(8,128)(2,1)}) %all-gather.2.cloned.1.call-update) | async-done | bytes 2359312 | tf_op jit(solution)/shard_map/all_gather | solution.py:34
  35.7 12.3 %fusion.29 = f32[192,2048]{1,0:T(8,128)} fusion(bf16[192,6144]{1,0:T(8,128)(2,1)} %all-gather.2.cloned.1.call-done, bf16[6144,2048]{1,0:T(8,128)(2,1)} %param.9), kind=kOutput, calls=%fused_computation.50 | convolution fusion | flops 4831838208 | bytes 29097984 | tf_op jit(solution)/shard_map/dot_general | solution.py:35
  48.9 34.6 %reduce-scatter.3.cloned.1.call-done = f32[192,512]{1,0:T(8,128)} async-done(((f32[192,2048]{1,0:T(8,128)}), f32[192,512]{1,0:T(8,128)}) %reduce-scatter.3.cloned.1.call-update) | async-done | bytes 393232 | tf_op jit(solution)/shard_map/reduce_scatter | solution.py:36
  83.5 1.0 convert_element_type.26
  84.9 8.6 %fusion.19 = f32[192,9216]{1,0:T(8,128)} fusion(bf16[512,9216]{1,0:T(8,128)(2,1)} %param.11, f32[192,512]{1,0:T(8,128)S(1)} %reshape.91, f32[512]{0:T(512)S(1)} %convert_element_type.27), kind=kOutput, calls=%fused_computation.28 | convolution fusion | flops 1812135936 | bytes 16910336 | tf_op jit(solution)/shard_map/dot_general | solution.py:46
  93.6 62.7 %reduce-scatter.5.cloned.1.call-done = f32[48,9216]{1,0:T(8,128)} async-done(((f32[192,9216]{1,0:T(8,128)}), f32[48,9216]{1,0:T(8,128)}) %reduce-scatter.5.cloned.1.call-update) | async-done | bytes 1769488 | tf_op jit(solution)/shard_map/reduce_scatter | solution.py:48
  156.4 3.1 fusion.27
  159.5 4.7 %copy.33 = bf16[6,128,1,512]{1,3,0,2:T(8,128)(2,1)} copy(bf16[6,128,1,512]{3,2,1,0:T(2,128)(2,1)} %get-tuple-element.5) | data formatting | bytes 1572864
  164.1 2.6 copy.34
  167.0 34.1 %psum.29 = f32[192]{0:T(256)S(1)} all-reduce(f32[192]{0:T(256)S(1)} %multiply_reduce_fusion), channel_id=1, replica_groups=mesh['groups'=2,'req'=4,'tensor'=4] {'req','tensor'}, use_global_device_ids=true, to_apply=%region_6.7 | all-reduce | flops 192 | bytes 1536 | tf_op jit(solution)/shard_map/psum | solution.py:50
  201.2 34.3 %all-reduce.3.cloned.1.call-done = f32[48,9216]{1,0:T(8,128)} async-done(((f32[48,9216]{1,0:T(8,128)}), f32[48,9216]{1,0:T(8,128)}) %all-reduce.3.cloned.1.call-update) | async-done | bytes 1769488 | tf_op jit(solution)/shard_map/psum | solution.py:54
  235.5 1.6 multiply_convert_fusion
  237.2 2.0 fusion.28
  239.1 0.6 bitcast_reduce_fusion
  239.8 18.5 %pmax.7 = f32[6,8,4,16]{3,1,2,0:T(8,128)S(1)} all-reduce(f32[6,8,4,16]{3,1,2,0:T(8,128)S(1)} %max.5), channel_id=1, replica_groups=mesh['groups'=2,'req'=4,'tensor'=4] {'tensor'}, use_global_device_ids=true, to_apply=%region_9.10 | all-reduce | flops 3072 | bytes 24576 | tf_op jit(solution)/shard_map/pmax | solution.py:96
  258.3 1.7 fusion.6
  260.0 1.8 bitcast_add_fusion
  261.8 0.6 copy-done.5
  263.1 0.9 fusion.4
  264.0 21.0 %psum.31 = f32[6,8,4,16]{3,1,2,0:T(8,128)S(1)} all-reduce(f32[6,8,4,16]{3,1,2,0:T(8,128)S(1)} %add.56), channel_id=1, replica_groups=mesh['groups'=2,'req'=4,'tensor'=4] {'tensor'}, use_global_device_ids=true, to_apply=%region_13.14 | all-reduce | flops 3072 | bytes 24576 | tf_op jit(solution)/shard_map/psum | solution.py:113
  285.0 46.5 %all-reduce.5.cloned.1.call-done = f32[6,8,4,16,128]{4,3,1,2,0:T(8,128)} async-done(((f32[6,8,4,16,128]{4,3,1,2,0:T(8,128)}), f32[6,8,4,16,128]{4,3,1,2,0:T(8,128)}) %all-reduce.5.cloned.1.call-update) | async-done | bytes 1572880 | tf_op jit(solution)/shard_map/psum | solution.py:113
  331.5 1.9 broadcast_divide_fusion
  334.0 0.8 select_convert_fusion
  (41 shorter events, 3.0 us)
Async XLA Ops:
  6.5 29.2 %all-gather.2.cloned.1.call-start = ((), (), s32[]{:S(2)}) async-start(), calls=%async_computation.2 | async-start | bytes 2949120 | tf_op jit(solution)/shard_map/all_gather | solution.py:34
  7.3 76.3 %reduce-scatter.3.cloned.1.call-start = ((), (), s32[]{:S(2)}) async-start(), calls=%async_computation.3 | async-start | bytes 1966080 | tf_op jit(solution)/shard_map/reduce_scatter | solution.py:36
  48.0 0.7 copy-start.2
  48.0 0.7 copy-start.3
  48.1 108.2 %reduce-scatter.5.cloned.1.call-start = ((), (), s32[]{:S(2)}) async-start(), calls=%async_computation.4 | async-start | bytes 8847360 | tf_op jit(solution)/shard_map/reduce_scatter | solution.py:48
  93.6 62.8 %copy-start = (bf16[6,128,2,512]{3,2,1,0:T(2,128)(2,1)S(1)}, bf16[6,128,2,512]{3,2,1,0:T(2,128)(2,1)}, u32[]{:S(2)}) copy-start(bf16[6,128,2,512]{3,2,1,0:T(2,128)(2,1)} %param.12) | copy-start | bytes 4718596
  93.6 141.9 %all-reduce.3.cloned.1.call-start = ((), (), s32[]{:S(2)}) async-start(), calls=%async_computation.5 | async-start | bytes 3538944 | tf_op jit(solution)/shard_map/psum | solution.py:54
  156.3 175.2 %all-reduce.5.cloned.1.call-start = ((), (), s32[]{:S(2)}) async-start(), calls=%async_computation.6 | async-start | bytes 3145728 | tf_op jit(solution)/shard_map/psum | solution.py:113
  164.1 2.6 copy-start.4
  237.1 2.0 copy-start.1
  261.8 0.7 copy-start.5
Sparse Core Ops, SparseCore 0:
  8.9 26.7 all-gather.1
  48.2 35.2 reduce-scatter.2
  93.7 62.5 reduce-scatter.4
  158.7 76.7 all-reduce.2
  261.9 69.5 all-reduce.4
where the time goes:
time: 342 us; the launch traced here: 341 us
  waiting for transfers between devices  207 us (61%)
  blocking collectives  73.6 us (22%)
  matrix products  27.2 us (8%)
  between operations  13.3 us (4%)
  local copies, waits for them, and re-layouts  12.5 us (4%)
  other arithmetic  7.31 us (2%)
    reduce_scatter x1, waiting for transfers between devices, body(): lax.psum_scatter(partial_qkv, 'req', scatter_dimension=0, tiled=True)  62.7 us
    psum x1, waiting for transfers between devices, body(): accum_all, denom_all = lax.psum((accum, denominator), 'tensor')  46.5 us
    reduce_scatter x1, waiting for transfers between devices, body(): lax.psum_scatter(partial_sum, 'tensor', scatter_dimension=1, tiled=True)  34.6 us
    psum x1, waiting for transfers between devices, body(): total_qkv = lax.psum(own_qkv, 'tensor')  34.3 us
    psum x1, blocking collectives, body(): lax.psum(row_squares, ('req', 'tensor'))  34.1 us
    all_gather x1, waiting for transfers between devices, body(): hidden_all = lax.all_gather(hidden, 'req', axis=0, tiled=True)  28.4 us
    psum x1, blocking collectives, body(): accum_all, denom_all = lax.psum((accum, denominator), 'tensor')  21 us
    pmax x1, blocking collectives, body(): top_score = lax.pmax(local_top, 'tensor')  18.5 us
  transfers between devices with their start and end apart: 5, of which 5 were waited for; matrix products, arithmetic and copies ran while one was open for 4% of the time, Pallas kernels for 0%

commit v1 on v0

--- a/solution.py
+++ b/solution.py
@@ -10,6 +10,15 @@
 TREE_SLOTS = 8
 CACHE_BLOCK = 128
 norm_eps = 1e-05
+spot_drive = lambda arr_in, which_axis, dimension_no: jnp.concatenate(
+    lax.all_to_all(
+        jnp.stack([arr_in for _ in range(lax.axis_size(which_axis))]),
+        axis_name=which_axis,
+        split_axis=0,
+        concat_axis=0,
+    ),
+    axis=dimension_no,
+)
 
 
 def slots(owner, request_per_owner):
@@ -31,7 +40,7 @@
     slot_of = slots(owner, request_per_owner)
     slot_table = slot_of[None, :] == jnp.arange(count_all, dtype=jnp.int32)[:, None]
     rows_all = count_all * TREE_SLOTS
-    hidden_all = lax.all_gather(hidden, "req", axis=0, tiled=True)
+    hidden_all = spot_drive(hidden, "req", 0)
     partial_sum = jnp.dot(hidden_all, join_weight, preferred_element_type=jnp.float32)
     joined = lax.psum_scatter(partial_sum, "tensor", scatter_dimension=1, tiled=True).astype(
         jnp.bfloat16

time: 342 us -> 347 us (1.015)
  blocking collectives: 73.6 us -> 106 us
  waiting for transfers between devices: 207 us -> 179 us
    all_to_all x0 -> x1, blocking collectives: none -> 32.5 us  [lax.all_to_all(jnp.stack([arr_in for _ in range(lax.axis_size(which_axis)...]
    all_gather x1 -> x0, waiting for transfers between devices: 28.4 us -> none  [body(): hidden_all = lax.all_gather(hidden, 'req', axis=0, tiled=True)]
  transfers between devices with their start and end apart: 5 -> 4, of which waited for: 5 -> 4; matrix products, arithmetic and copies ran while one was open for 4% -> 4% of each run, Pallas kernels for 0% -> 0%
where the time goes in v1:
time: 347 us; the launch traced here: 346 us
  waiting for transfers between devices  179 us (52%)
  blocking collectives  106 us (31%)
  matrix products  26.9 us (8%)
  local copies, waits for them, and re-layouts  13.8 us (4%)
  between operations  13.3 us (4%)
  other arithmetic  7.31 us (2%)
    reduce_scatter x1, waiting for transfers between devices, body(): lax.psum_scatter(partial_qkv, 'req', scatter_dimension=0, tiled=True)  62.8 us
    psum x1, waiting for transfers between devices, body(): accum_all, denom_all = lax.psum((accum, denominator), 'tensor')  46.5 us
    reduce_scatter x1, waiting for transfers between devices, body(): lax.psum_scatter(partial_sum, 'tensor', scatter_dimension=1, tiled=True)  34.9 us
    psum x1, waiting for transfers between devices, body(): total_qkv = lax.psum(own_qkv, 'tensor')  34.4 us
    psum x1, blocking collectives, body(): lax.psum(row_squares, ('req', 'tensor'))  34.1 us
    all_to_all x1, blocking collectives, lax.all_to_all(jnp.stack([arr_in for _ in range(lax.axis_size(which_axis)...  32.5 us
    psum x1, blocking collectives, body(): accum_all, denom_all = lax.psum((accum, denominator), 'tensor')  21 us
    pmax x1, blocking collectives, body(): top_score = lax.pmax(local_top, 'tensor')  18.4 us
  transfers between devices with their start and end apart: 4, of which 4 were waited for; matrix products, arithmetic and copies ran while one was open for 4% of the time, Pallas kernels for 0%

profile of v1, /device:TPU:0, one launch (start us, length us, event | category | flops | bytes accessed | tf_op | source)
XLA Modules:
  0.0 346.2 jit_solution(4760492322875015030)
XLA Ops:
  6.5 1.3 stack.2
  7.9 32.5 %all_to_all.5 = bf16[4,48,6144]{2,1,0:T(8,128)(2,1)S(1)} all-to-all(bf16[4,48,6144]{2,1,0:T(8,128)(2,1)S(1)} %stack.2), channel_id=1, replica_groups=mesh['groups'=2,'req'=4,'tensor'=4] {'req'}, dimensions={0} | all-to-all | bytes 4718592 | tf_op jit(solution)/shard_map/all_to_all | solution.py:14
  40.4 12.0 %fusion.29 = f32[192,2048]{1,0:T(8,128)} fusion(bf16[192,6144]{1,0:T(8,128)(2,1)S(1)} %bitcast.60, bf16[6144,2048]{1,0:T(8,128)(2,1)} %param.9), kind=kOutput, calls=%fused_computation.50 | convolution fusion | flops 4831838208 | bytes 29097984 | tf_op jit(solution)/shard_map/dot_general | solution.py:44
  53.2 34.9 %reduce-scatter.3.cloned.1.call-done = f32[192,512]{1,0:T(8,128)} async-done(((f32[192,2048]{1,0:T(8,128)}), f32[192,512]{1,0:T(8,128)}) %reduce-scatter.3.cloned.1.call-update) | async-done | bytes 393232 | tf_op jit(solution)/shard_map/reduce_scatter | solution.py:45
  88.2 1.0 convert_element_type.26
  89.6 8.6 %fusion.19 = f32[192,9216]{1,0:T(8,128)} fusion(bf16[512,9216]{1,0:T(8,128)(2,1)} %param.11, f32[192,512]{1,0:T(8,128)S(1)} %reshape.97, f32[512]{0:T(512)S(1)} %convert_element_type.27), kind=kOutput, calls=%fused_computation.28 | convolution fusion | flops 1812135936 | bytes 16910336 | tf_op jit(solution)/shard_map/dot_general | solution.py:55
  98.3 62.8 %reduce-scatter.5.cloned.1.call-done = f32[48,9216]{1,0:T(8,128)} async-done(((f32[192,9216]{1,0:T(8,128)}), f32[48,9216]{1,0:T(8,128)}) %reduce-scatter.5.cloned.1.call-update) | async-done | bytes 1769488 | tf_op jit(solution)/shard_map/reduce_scatter | solution.py:57
  161.2 3.1 fusion.27
  164.2 4.7 %copy.33 = bf16[6,128,1,512]{1,3,0,2:T(8,128)(2,1)} copy(bf16[6,128,1,512]{3,2,1,0:T(2,128)(2,1)} %get-tuple-element.5) | data formatting | bytes 1572864
  168.9 2.6 copy.34
  171.8 34.1 %psum.29 = f32[192]{0:T(256)S(1)} all-reduce(f32[192]{0:T(256)S(1)} %multiply_reduce_fusion), channel_id=1, replica_groups=mesh['groups'=2,'req'=4,'tensor'=4] {'req','tensor'}, use_global_device_ids=true, to_apply=%region_6.7 | all-reduce | flops 192 | bytes 1536 | tf_op jit(solution)/shard_map/psum | solution.py:59
  206.0 34.4 %all-reduce.3.cloned.1.call-done = f32[48,9216]{1,0:T(8,128)} async-done(((f32[48,9216]{1,0:T(8,128)}), f32[48,9216]{1,0:T(8,128)}) %all-reduce.3.cloned.1.call-update) | async-done | bytes 1769488 | tf_op jit(solution)/shard_map/psum | solution.py:63
  240.4 1.6 multiply_convert_fusion
  242.1 2.0 fusion.28
  244.1 0.6 bitcast_reduce_fusion
  244.8 18.4 %pmax.7 = f32[6,8,4,16]{3,1,2,0:T(8,128)S(1)} all-reduce(f32[6,8,4,16]{3,1,2,0:T(8,128)S(1)} %max.5), channel_id=1, replica_groups=mesh['groups'=2,'req'=4,'tensor'=4] {'tensor'}, use_global_device_ids=true, to_apply=%region_9.10 | all-reduce | flops 3072 | bytes 24576 | tf_op jit(solution)/shard_map/pmax | solution.py:105
  263.2 1.7 fusion.6
  264.9 1.8 bitcast_add_fusion
  266.7 0.6 copy-done.5
  268.0 0.9 fusion.4
  269.0 21.0 %psum.31 = f32[6,8,4,16]{3,1,2,0:T(8,128)S(1)} all-reduce(f32[6,8,4,16]{3,1,2,0:T(8,128)S(1)} %add.56), channel_id=1, replica_groups=mesh['groups'=2,'req'=4,'tensor'=4] {'tensor'}, use_global_device_ids=true, to_apply=%region_13.14 | all-reduce | flops 3072 | bytes 24576 | tf_op jit(solution)/shard_map/psum | solution.py:122
  289.9 46.5 %all-reduce.5.cloned.1.call-done = f32[6,8,4,16,128]{4,3,1,2,0:T(8,128)} async-done(((f32[6,8,4,16,128]{4,3,1,2,0:T(8,128)}), f32[6,8,4,16,128]{4,3,1,2,0:T(8,128)}) %all-reduce.5.cloned.1.call-update) | async-done | bytes 1572880 | tf_op jit(solution)/shard_map/psum | solution.py:122
  336.5 1.9 broadcast_divide_fusion
  338.9 0.8 select_convert_fusion
  (40 shorter events, 3.0 us)
Async XLA Ops:
  6.5 81.6 %reduce-scatter.3.cloned.1.call-start = ((), (), s32[]{:S(2)}) async-start(), calls=%async_computation.3 | async-start | bytes 1966080 | tf_op jit(solution)/shard_map/reduce_scatter | solution.py:45
  52.4 0.7 copy-start.2
  52.4 0.7 copy-start.3
  52.4 108.7 %reduce-scatter.5.cloned.1.call-start = ((), (), s32[]{:S(2)}) async-start(), calls=%async_computation.4 | async-start | bytes 8847360 | tf_op jit(solution)/shard_map/reduce_scatter | solution.py:57
  98.2 62.9 %copy-start = (bf16[6,128,2,512]{3,2,1,0:T(2,128)(2,1)S(1)}, bf16[6,128,2,512]{3,2,1,0:T(2,128)(2,1)}, u32[]{:S(2)}) copy-start(bf16[6,128,2,512]{3,2,1,0:T(2,128)(2,1)} %param.12) | copy-start | bytes 4718596
  98.2 142.2 %all-reduce.3.cloned.1.call-start = ((), (), s32[]{:S(2)}) async-start(), calls=%async_computation.5 | async-start | bytes 3538944 | tf_op jit(solution)/shard_map/psum | solution.py:63
  161.1 175.4 %all-reduce.5.cloned.1.call-start = ((), (), s32[]{:S(2)}) async-start(), calls=%async_computation.6 | async-start | bytes 3145728 | tf_op jit(solution)/shard_map/psum | solution.py:122
  168.9 2.6 copy-start.4
  242.1 2.0 copy-start.1
  266.7 0.7 copy-start.5
Sparse Core Ops, SparseCore 0:
  52.5 35.6 reduce-scatter.2
  98.3 62.6 reduce-scatter.4
  163.6 76.7 all-reduce.2
  266.9 69.5 all-reduce.4
